TPU v7x, 32 devices: a whole 2x2x4 slice. The times are simulated.
32 devices in a mesh: row: 8 (over z, y), col: 4 (over x, core).
Axes of the slice: x: 2, y: 2, z: 4, core: 2. Of those that a mesh axis runs over, the one named last changes fastest.
Arguments:
- anc_factor: float32 [8192, 4096], P('row', 'col'), may hold values from -0.09375 to 0.09375
- anc_solution: float32 [128, 12288], P('col', 'row'), may hold values from -6 to 6
- slot_row: int32 [8192], P('row'), may hold values from 0 to 1535, as said below
- tile_count: int32 [8], P('row'), may hold values from 2 to 8, as said below
- lower_factor: float32 [4, 1024, 4096], P(None, 'row', 'col'), may hold values from -0.109375 to 0.109375
- diag_inverse: float32 [4, 1024, 1024], P('col'), may hold values from -1.5 to 1.5, as said below
- rhs: float32 [128, 4096], P('row', 'col'), may hold values from -6 to 6
Outputs:
- solution: float32 [128, 4096], P('row', 'col')
Inputs may be any that keep to these rules, and one draw needn't show every extreme that they name: `slot_row`: within each aligned block of 1024 entries the values are distinct, and some block holds 1535. `tile_count`: some entry equals 8 in every draw. Each block diag_inverse[t] is lower triangular with a positive diagonal.
All inputs are finite; a program needn't handle non-finite values.
Results may differ from a plain program's by a relative error of at most 0.0001.
Values sent between devices are 32-bit elements; how exact they have to be, the bound alone decides.
A program may use at most 64 MiB of HBM per device.

v0:
```python
import jax
import jax.numpy as jnp
from jax import lax
from jax.sharding import PartitionSpec as P

TILE = 128


def broadcast(array, axis, root):
    mine = lax.axis_index(axis) == root
    return lax.psum(jnp.where(mine, array, jnp.zeros_like(array)), axis)


def on_device(anc_factor, anc_solution, slot_row, tile_count, lower_factor, diag_inverse, rhs):
    highest = lax.Precision.HIGHEST
    column_index = lax.axis_index("col")
    panels = lower_factor.shape[0]
    rows_local = lower_factor.shape[1]
    slot_total = slot_row.shape[0]
    alive_mask = (jnp.arange(slot_total) < tile_count[0] * TILE).astype(jnp.float32)
    selected = jnp.take(anc_solution, slot_row, axis=1) * alive_mask[None, :]
    ancestor_term = jnp.dot(
        lax.all_gather(selected, "col", axis=0, tiled=True),
        anc_factor,
        precision=highest,
        preferred_element_type=jnp.float32,
    )
    reduced = rhs - lax.psum_scatter(ancestor_term, "row", scatter_dimension=0, tiled=True)
    pending = jnp.zeros_like(reduced)
    result = jnp.zeros_like(reduced)
    panel_mask = (jnp.arange(panels) > column_index).astype(jnp.float32)
    lower_masked = lower_factor * panel_mask[:, None, None]
    lower_flat = lower_masked.reshape(panels * rows_local, lower_factor.shape[2])
    all_rhs = anc_solution.shape[0] * lax.axis_size("col")
    known_rows = jnp.zeros((all_rhs, panels * rows_local), jnp.float32)
    for target in range(panels - 1, -1, -1):
        if target < panels - 1:
            partial_sum = jnp.dot(
                known_rows, lower_flat, precision=highest, preferred_element_type=jnp.float32
            )
            pending = lax.psum_scatter(partial_sum, "row", scatter_dimension=0, tiled=True)
        solved = jnp.dot(
            reduced - pending,
            diag_inverse[0],
            precision=highest,
            preferred_element_type=jnp.float32,
        )
        result = jnp.where(column_index == target, solved, result)
        if target > 0:
            spread_rows = lax.all_to_all(solved, "row", split_axis=1, concat_axis=0, tiled=True)
            owner_rows = broadcast(spread_rows, "col", target)
            known_rows = known_rows.at[:, target * rows_local : (target + 1) * rows_local].set(
                owner_rows
            )
    return result


def solution(mesh):
    in_specs = (
        P("row", "col"),
        P("col", "row"),
        P("row"),
        P("row"),
        P(None, "row", "col"),
        P("col", None, None),
        P("row", "col"),
    )
    out_specs = P("row", "col")
    return jax.shard_map(
        on_device, mesh=mesh, in_specs=in_specs, out_specs=out_specs, check_vma=False
    )
```

profile of v0, /device:TPU:0, one launch (start us, length us, event | category | flops | bytes accessed | tf_op | source)
XLA Modules:
  0.0 433.6 jit_solution(18355791746829036453)
XLA Ops:
  9.8 2.8 gather_fusion
  13.1 8.6 %all_gather.3 = f32[128,1024]{1,0:T(8,128)S(1)} all-gather(f32[32,1024]{1,0:T(8,128)S(1)} %copy.14), channel_id=1, replica_groups=mesh['row'=8,'col'=4] {'col'}, dimensions={0}, use_global_device_ids=true | all-gather | bytes 655360 | tf_op jit(solution)/shard_map/all_gather | solution.py:23
  21.7 5.4 %fusion.20 = f32[128,1024]{1,0:T(8,128)} fusion(f32[128,1024]{1,0:T(8,128)S(1)} %all_gather.3, f32[1024,1024]{1,0:T(8,128)} %param.13), kind=kOutput, calls=%fused_computation.36 | convolution fusion | flops 1610612736 | bytes 5242880 | tf_op jit(solution)/shard_map/dot_general | solution.py:22
  27.1 63.0 %reduce-scatter.5.cloned.1.call-done = f32[16,1024]{1,0:T(8,128)} async-done(((f32[128,1024]{1,0:T(8,128)}), f32[16,1024]{1,0:T(8,128)}) %reduce-scatter.5.cloned.1.call-update) | async-done | bytes 65552 | tf_op jit(solution)/shard_map/reduce_scatter | solution.py:28
  91.0 4.3 fusion.6
  95.9 3.6 all-to-all-start
  99.5 6.8 %all-to-all-done = f32[16,8,128]{2,0,1:T(8,128)S(1)} async-done(((f32[16,8,128]{2,0,1:T(8,128)}), f32[16,8,128]{2,0,1:T(8,128)S(1)}, u32[]{:S(2)}, u32[]{:S(2)}) %all-to-all-start) | async-done | bytes 65568 | tf_op jit(solution)/shard_map/all_to_all | solution.py:50
  107.1 1.9 broadcast_multiply_fusion
  109.0 26.7 %all-reduce.5.cloned.1.call-done = f32[128,128]{1,0:T(8,128)} async-done(((f32[128,128]{1,0:T(8,128)}), f32[128,128]{1,0:T(8,128)}) %all-reduce.5.cloned.1.call-update) | async-done | bytes 65552 | tf_op jit(solution)/shard_map/psum | solution.py:11
  135.7 3.0 fusion.11
  138.7 62.3 %reduce-scatter.7.cloned.1.call-done = f32[16,1024]{1,0:T(8,128)} async-done(((f32[128,1024]{1,0:T(8,128)}), f32[16,1024]{1,0:T(8,128)}) %reduce-scatter.7.cloned.1.call-update) | async-done | bytes 65552 | tf_op jit(solution)/shard_map/reduce_scatter | solution.py:41
  201.0 4.3 fusion.4
  206.0 3.6 all-to-all-start.1
  209.6 6.9 %all-to-all-done.1 = f32[16,8,128]{2,0,1:T(8,128)S(1)} async-done(((f32[16,8,128]{2,0,1:T(8,128)}), f32[16,8,128]{2,0,1:T(8,128)S(1)}, u32[]{:S(2)}, u32[]{:S(2)}) %all-to-all-start.1) | async-done | bytes 65568 | tf_op jit(solution)/shard_map/all_to_all | solution.py:50
  218.0 27.8 %all-reduce.7.cloned.1.call-done = f32[128,128]{1,0:T(8,128)} async-done(((f32[128,128]{1,0:T(8,128)}), f32[128,128]{1,0:T(8,128)}) %all-reduce.7.cloned.1.call-update) | async-done | bytes 65552 | tf_op jit(solution)/shard_map/psum | solution.py:11
  247.3 2.1 fusion.21
  249.4 62.1 %reduce-scatter.9.cloned.1.call-done = f32[16,1024]{1,0:T(8,128)} async-done(((f32[128,1024]{1,0:T(8,128)}), f32[16,1024]{1,0:T(8,128)}) %reduce-scatter.9.cloned.1.call-update) | async-done | bytes 65552 | tf_op jit(solution)/shard_map/reduce_scatter | solution.py:41
  311.4 4.3 fusion.2
  316.4 3.6 all-to-all-start.2
  320.0 6.9 %all-to-all-done.2 = f32[16,8,128]{2,0,1:T(8,128)S(1)} async-done(((f32[16,8,128]{2,0,1:T(8,128)}), f32[16,8,128]{2,0,1:T(8,128)S(1)}, u32[]{:S(2)}, u32[]{:S(2)}) %all-to-all-start.2) | async-done | bytes 65568 | tf_op jit(solution)/shard_map/all_to_all | solution.py:50
  328.2 28.0 %all-reduce.9.cloned.1.call-done = f32[128,128]{1,0:T(8,128)} async-done(((f32[128,128]{1,0:T(8,128)}), f32[128,128]{1,0:T(8,128)}) %all-reduce.9.cloned.1.call-update) | async-done | bytes 65552 | tf_op jit(solution)/shard_map/psum | solution.py:11
  357.7 2.1 fusion.22
  359.8 62.0 %reduce-scatter.11.cloned.1.call-done = f32[16,1024]{1,0:T(8,128)} async-done(((f32[128,1024]{1,0:T(8,128)}), f32[16,1024]{1,0:T(8,128)}) %reduce-scatter.11.cloned.1.call-update) | async-done | bytes 65552 | tf_op jit(solution)/shard_map/reduce_scatter | solution.py:41
  421.8 4.9 %fusion.8 = f32[16,1024]{1,0:T(8,128)} fusion(f32[1,1024,1024]{2,1,0:T(8,128)} %param.18, f32[16,1024]{1,0:T(8,128)S(1)} %fusion.2, f32[16,1024]{1,0:T(8,128)S(1)} %fusion.4, f32[16,1024]{1,0:T(8,128)S(1)} %fusion.6, f32[16,1024]{1,0:T(8,128)S(1)} %sub.12, f32[16,1024]{1,0:T(8,128)} %reduce-scatter.11.cloned.1.call-done, pred[]{:T(512)S(6)} %eq.16, ...), kind=kOutput, calls=%fused_computation.9 | convolution fusion | flops 201408512 | bytes 4587524 | tf_op jit(solution)/shard_map/dot_general | solution.py:42
  (36 shorter events, 12.4 us)
Async XLA Ops:
  6.5 83.6 %reduce-scatter.5.cloned.1.call-start = ((), (), s32[]{:S(2)}) async-start(), calls=%async_computation.7 | async-start | bytes 589824 | tf_op jit(solution)/shard_map/reduce_scatter | solution.py:28
  12.6 77.5 %copy-start.1 = (f32[16,1024]{1,0:T(8,128)S(1)}, f32[16,1024]{1,0:T(8,128)}, u32[]{:S(2)}) copy-start(f32[16,1024]{1,0:T(8,128)} %param.19) | copy-start | bytes 196612
  95.9 10.5 %all-to-all-start = ((f32[16,8,128]{2,0,1:T(8,128)}), f32[16,8,128]{2,0,1:T(8,128)S(1)}, u32[]{:S(2)}, u32[]{:S(2)}) async-start(f32[16,8,128]{2,0,1:T(8,128)} %copy_bitcast_fusion.2), calls=%async_computation.1 | async-start | bytes 131072 | tf_op jit(solution)/shard_map/all_to_all | solution.py:50
  99.5 36.2 %all-reduce.5.cloned.1.call-start = ((), (), s32[]{:S(2)}) async-start(), calls=%async_computation.8 | async-start | bytes 131072 | tf_op jit(solution)/shard_map/psum | solution.py:11
  107.1 94.0 %reduce-scatter.7.cloned.1.call-start = ((), (), s32[]{:S(2)}) async-start(), calls=%async_computation.9 | async-start | bytes 589824 | tf_op jit(solution)/shard_map/reduce_scatter | solution.py:41
  135.7 82.3 %copy-start = (f32[128,128]{1,0:T(8,128)S(1)}, f32[128,128]{1,0:T(8,128)}, u32[]{:S(2)}) copy-start(f32[128,128]{1,0:T(8,128)} %all-reduce.5.cloned.1.call-done) | copy-start | bytes 196612
  206.0 10.5 %all-to-all-start.1 = ((f32[16,8,128]{2,0,1:T(8,128)}), f32[16,8,128]{2,0,1:T(8,128)S(1)}, u32[]{:S(2)}, u32[]{:S(2)}) async-start(f32[16,8,128]{2,0,1:T(8,128)} %copy_bitcast_fusion.1), calls=%async_computation.3 | async-start | bytes 131072 | tf_op jit(solution)/shard_map/all_to_all | solution.py:50
  209.6 36.3 %all-reduce.7.cloned.1.call-start = ((), (), s32[]{:S(2)}) async-start(), calls=%async_computation.10 | async-start | bytes 131072 | tf_op jit(solution)/shard_map/psum | solution.py:11
  217.1 94.3 %reduce-scatter.9.cloned.1.call-start = ((), (), s32[]{:S(2)}) async-start(), calls=%async_computation.11 | async-start | bytes 589824 | tf_op jit(solution)/shard_map/reduce_scatter | solution.py:41
  316.4 10.5 %all-to-all-start.2 = ((f32[16,8,128]{2,0,1:T(8,128)}), f32[16,8,128]{2,0,1:T(8,128)S(1)}, u32[]{:S(2)}, u32[]{:S(2)}) async-start(f32[16,8,128]{2,0,1:T(8,128)} %copy_bitcast_fusion), calls=%async_computation.5 | async-start | bytes 131072 | tf_op jit(solution)/shard_map/all_to_all | solution.py:50
  320.0 36.3 %all-reduce.9.cloned.1.call-start = ((), (), s32[]{:S(2)}) async-start(), calls=%async_computation.12 | async-start | bytes 131072 | tf_op jit(solution)/shard_map/psum | solution.py:11
  327.6 94.2 %reduce-scatter.11.cloned.1.call-start = ((), (), s32[]{:S(2)}) async-start(), calls=%async_computation.13 | async-start | bytes 589824 | tf_op jit(solution)/shard_map/reduce_scatter | solution.py:41
Sparse Core Ops, SparseCore 0:
  27.3 62.8 reduce-scatter.4
  107.2 28.5 all-reduce.4
  139.1 61.9 reduce-scatter.6
  217.3 28.5 all-reduce.6
  249.5 61.9 reduce-scatter.8
  327.7 28.5 all-reduce.8
  359.9 61.8 reduce-scatter.10
where the time goes:
time: 434 us
  waiting for transfers between devices  353 us (81%)
  matrix products  30.3 us (7%)
  between operations  14.2 us (3%)
  starting transfers between devices  11.2 us (3%)
  other arithmetic  10.5 us (2%)
  blocking collectives  8.61 us (2%)
  local copies, waits for them, and re-layouts  6.1 us (1%)
    reduce_scatter x3, waiting for transfers between devices, on_device(): lax.psum_scatter(partial_sum, 'row', scatter_dimension=0, tiled=True)  186 us
    psum x3, waiting for transfers between devices, broadcast(): return lax.psum(jnp.where(mine, array, jnp.zeros_like(array)), axis)  82.6 us
    reduce_scatter x1, waiting for transfers between devices, on_device(): lax.psum_scatter(ancestor_term, 'row', scatter_dimension=0, tiled=True)  63 us
    all_to_all x3, waiting for transfers between devices, on_device(): lax.all_to_all(solved, 'row', split_axis=1, concat_axis=0, tiled=True)  20.6 us
    dot_general x4, matrix products, on_device(): jnp.dot(reduced - pending, diag_inverse[0], precision=highest, preferred_...  17.8 us
    all_to_all x3, starting transfers between devices, on_device(): lax.all_to_all(solved, 'row', split_axis=1, concat_axis=0, tiled=True)  10.8 us
  transfers between devices with their start and end apart: 10, of which 10 were waited for; matrix products, arithmetic and copies ran while one was open for 1% of the time, Pallas kernels for 0%

commit v1 on v0

v1 whole, which is shorter than its diff:
```python
import functools

import jax
import jax.numpy as jnp
from jax import lax
from jax.experimental import pallas as pl
from jax.experimental.pallas import tpu as pltpu
from jax.sharding import PartitionSpec as P

TILE = 128
LANES = 128
MESH = pl.DeviceIdType.MESH
F32 = jnp.float32
BF16 = jnp.bfloat16


def split(x):
    hi = x.astype(BF16)
    lo = (x - hi.astype(F32)).astype(BF16)
    return hi, lo


def mm(a, b):
    return jnp.dot(a, b, preferred_element_type=F32)


def kernel(
    group,
    n_row,
    n_col,
    slot_ref,
    count_ref,
    parent_ref,
    rhs_ref,
    anc_ref,
    low_ref,
    diag_ref,
    out_ref,
    anc_f,
    anc_h,
    anc_l,
    diag_f,
    diag_h,
    diag_l,
    low_all,
    low_s,
    fold_h,
    fold_l,
    par_s,
    sel,
    sel_s,
    part,
    part_in,
    pre_s,
    acc,
    red_in,
    solved,
    x_in,
    x_s,
    sem_anc,
    sem_diag,
    sem_low,
    sel_tx,
    sel_rx,
    low_tx,
    low_rx,
    part_tx,
    part_rx,
    red_tx,
    red_rx,
    x_tx,
    x_rx,
):
    row = lax.axis_index("row")
    col = lax.axis_index("col")
    n_z = n_row // group
    z = row // group
    y = row % group
    width = diag_f.shape[1]
    slots = sel.shape[2]
    share = rhs_ref.shape[0]
    n_rhs = share * n_row
    sub = share * n_z
    wide = min(256, width)
    steps = width // wide
    depth = x_in.shape[3]

    copy_anc = pltpu.make_async_copy(anc_ref, anc_f, sem_anc)
    copy_anc.start()
    copy_diag = pltpu.make_async_copy(diag_ref.at[0], diag_f, sem_diag)
    copy_diag.start()
    for k in range(1, n_col):
        pltpu.make_async_copy(low_ref.at[k], low_all.at[k, y], sem_low.at[k]).start()

    barrier = pltpu.get_barrier_semaphore()

    def greet(dev_row, dev_col):
        pl.semaphore_signal(barrier, inc=1, device_id=(dev_row, dev_col), device_id_type=MESH)

    for d in range(n_z):
        for e in range(n_col):
            if d or e:
                greet(lax.rem(z + d, n_z) * group + y, lax.rem(col + e, n_col))
    for d in range(1, group):
        greet(z * group + lax.rem(y + d, group), col)

    mine = sel.shape[1]
    hi, lo = split(parent_ref[...])
    par_s[0:mine, :] = hi
    par_s[mine:, :] = lo
    parents = parent_ref.shape[1]

    def select(n, carry):
        at = pl.ds(pl.multiple_of(n * wide, wide), wide)
        place = lax.broadcasted_iota(jnp.int32, (1, wide), 1) + n * wide
        wanted = jnp.where(place < count_ref[0] * TILE, slot_ref[:, at], -1)
        which = lax.broadcasted_iota(jnp.int32, (parents, wide), 0)
        hot = jnp.where(which == wanted, 1.0, 0.0).astype(BF16)
        both = mm(par_s[...], hot)
        sel[col, :, at] = both[0:mine] + both[mine:]
        return carry

    lax.fori_loop(0, slots // wide, select, 0)

    pl.semaphore_wait(barrier, n_z * n_col - 1 + group - 1)

    def sel_copy(owner, to):
        return pltpu.make_async_remote_copy(
            src_ref=sel.at[owner],
            dst_ref=sel.at[owner],
            send_sem=sel_tx.at[to],
            recv_sem=sel_rx.at[owner],
            device_id=(row, to),
            device_id_type=MESH,
        )

    def others_col(e):
        return lax.rem(col + e, n_col)

    for e in range(1, n_col):
        sel_copy(col, others_col(e)).start()

    def low_copy(k, owner, to):
        return pltpu.make_async_remote_copy(
            src_ref=low_ref.at[k],
            dst_ref=low_all.at[k, owner],
            send_sem=low_tx.at[k, to],
            recv_sem=low_rx.at[k, owner],
            device_id=(z * group + to, col),
            device_id_type=MESH,
        )

    for k in range(n_col - 1, 0, -1):

        @pl.when(col < k)
        def _():
            for d in range(1, group):
                low_copy(k, y, lax.rem(y + d, group)).start()

    def split_rows(src, dst_h, dst_l):
        rows = 128

        def body(i, carry):
            at = pl.ds(pl.multiple_of(i * rows, rows), rows)
            h, l = split(src[at, :])
            dst_h[at, :] = h
            dst_l[at, :] = l
            return carry

        lax.fori_loop(0, src.shape[0] // rows, body, 0)

    copy_anc.wait()
    split_rows(anc_f, anc_h, anc_l)

    for e in range(1, n_col):
        sel_copy(others_col(e), col).wait_recv()
    hi, lo = split(sel[...].reshape(n_rhs, slots))
    sel_s[0:n_rhs, :] = hi
    sel_s[n_rhs:, :] = lo
    for n in range(steps):
        at = slice(n * wide, (n + 1) * wide)
        both = mm(sel_s[...], anc_h[:, at])
        term = both[0:n_rhs] + both[n_rhs:] + mm(sel_s[0:n_rhs, :], anc_l[:, at])
        for r in range(n_row):
            part[r % group, r // group, :, at] = term[r * share : (r + 1) * share]

    def part_copy(owner, to):
        return pltpu.make_async_remote_copy(
            src_ref=part.at[to],
            dst_ref=part_in.at[owner],
            send_sem=part_tx.at[to],
            recv_sem=part_rx.at[owner],
            device_id=(z * group + to, col),
            device_id_type=MESH,
        )

    for d in range(1, group):
        part_copy(y, lax.rem(y + d, group)).start()

    copy_diag.wait()
    split_rows(diag_f, diag_h, diag_l)

    for d in range(1, group):
        part_copy(lax.rem(y + d, group), y).wait_recv()

    pre = part[y]
    for d in range(1, group):
        pre = pre + part_in[lax.rem(y + d, group)]
    zs = lax.broadcasted_iota(jnp.int32, (n_z, 1, 1), 0)
    pre = jnp.where(zs == z, rhs_ref[...][None], 0.0) - pre
    hi, lo = split(pre.reshape(sub, width))
    pre_s[0:sub, :] = hi
    pre_s[sub:, :] = lo
    for n in range(steps):
        at = slice(n * wide, (n + 1) * wide)
        below = slice(n * wide, width)
        both = mm(pre_s[:, below], diag_h[below, at])
        term = both[0:sub] + both[sub:] + mm(pre_s[0:sub, below], diag_l[below, at])
        acc[:, :, at] = term.reshape(n_z, share, wide)

    for k in range(1, n_col):
        pltpu.make_async_copy(low_ref.at[k], low_all.at[k, y], sem_low.at[k]).wait()

    def fold(i, carry):
        k = n_col - 1 - i
        for d in range(1, group):
            low_copy(k, lax.rem(y + d, group), y).wait_recv()
        h, l = split(low_all[k].reshape(depth, width))
        low_s[0:depth, :] = h
        low_s[depth:, :] = l
        for n in range(steps):
            at = slice(n * wide, (n + 1) * wide)
            below = slice(n * wide, width)
            both = mm(low_s[:, below], diag_h[below, at])
            term = both[0:depth] + both[depth:] + mm(low_s[0:depth, below], diag_l[below, at])
            h, l = split(term)
            fold_h[k, :, at] = h
            fold_l[k, :, at] = l
        return carry

    lax.fori_loop(0, n_col - 1 - col, fold, 0)

    def x_copy(k, owner, to, to_col):
        return pltpu.make_async_remote_copy(
            src_ref=solved.at[:, pl.ds(pl.multiple_of(to * depth, depth), depth)],
            dst_ref=x_in.at[k, owner],
            send_sem=x_tx.at[to_col, to],
            recv_sem=x_rx.at[k, owner],
            device_id=(to * group + y, to_col),
            device_id_type=MESH,
        )

    def absorb(i, carry):
        k = n_col - 1 - i
        for d in range(n_z):
            x_copy(k, d, z, col).wait_recv()
        h, l = split(x_in[k].reshape(sub, depth))
        x_s[0:sub, :] = h
        x_s[sub:, :] = l
        for n in range(steps):
            at = slice(n * wide, (n + 1) * wide)
            both = mm(x_s[...], fold_h[k, :, at])
            term = both[0:sub] + both[sub:] + mm(x_s[0:sub, :], fold_l[k, :, at])
            acc[:, :, at] = acc[:, :, at] - term.reshape(n_z, share, wide)
        return carry

    lax.fori_loop(0, n_col - 1 - col, absorb, 0)

    def red_copy(owner, to):
        return pltpu.make_async_remote_copy(
            src_ref=acc.at[to],
            dst_ref=red_in.at[owner],
            send_sem=red_tx.at[to],
            recv_sem=red_rx.at[owner],
            device_id=(to * group + y, col),
            device_id_type=MESH,
        )

    for d in range(1, n_z):
        red_copy(z, lax.rem(z + d, n_z)).start()
    total = acc[z]
    for d in range(1, n_z):
        at = lax.rem(z + d, n_z)
        red_copy(at, z).wait_recv()
        total = total + red_in[at]
    solved[...] = total

    def spread(i, carry):
        to_col = col - 1 - i
        for d in range(n_z):
            x_copy(col, z, lax.rem(z + d, n_z), to_col).start()
        return carry

    lax.fori_loop(0, col, spread, 0)
    out_ref[...] = total

    def spread_done(i, carry):
        to_col = col - 1 - i
        for d in range(n_z):
            x_copy(col, z, lax.rem(z + d, n_z), to_col).wait_send()
        return carry

    lax.fori_loop(0, col, spread_done, 0)
    for d in range(1, n_z):
        red_copy(z, lax.rem(z + d, n_z)).wait_send()
    for d in range(1, group):
        part_copy(y, lax.rem(y + d, group)).wait_send()
    for e in range(1, n_col):
        sel_copy(col, others_col(e)).wait_send()
    for k in range(n_col - 1, 0, -1):

        @pl.when(col < k)
        def _():
            for d in range(1, group):
                low_copy(k, y, lax.rem(y + d, group)).wait_send()


def on_device(
    n_row, n_col, anc_factor, anc_solution, slot_row, tile_count, lower_factor, diag_inverse, rhs
):
    panels, rows_local, width = lower_factor.shape
    slots = slot_row.shape[0]
    share = rhs.shape[0]
    n_rhs = share * n_row
    group = max(2, LANES // rows_local)
    n_z = n_row // group
    depth = group * rows_local
    sub = share * n_z
    mine, parents = anc_solution.shape
    dma = pltpu.SemaphoreType.DMA
    vmem = pltpu.VMEM
    in_vmem = pl.BlockSpec(memory_space=pltpu.VMEM)
    anywhere = pl.BlockSpec(memory_space=pl.ANY)
    return pl.pallas_call(
        functools.partial(kernel, group, n_row, n_col),
        out_shape=jax.ShapeDtypeStruct(rhs.shape, F32),
        in_specs=[
            in_vmem,
            pl.BlockSpec(memory_space=pltpu.SMEM),
            in_vmem,
            in_vmem,
            anywhere,
            anywhere,
            anywhere,
        ],
        out_specs=in_vmem,
        scratch_shapes=[
            vmem((slots, width), F32),
            vmem((slots, width), BF16),
            vmem((slots, width), BF16),
            vmem((width, width), F32),
            vmem((width, width), BF16),
            vmem((width, width), BF16),
            vmem((panels, group, rows_local, width), F32),
            vmem((2 * depth, width), BF16),
            vmem((panels, depth, width), BF16),
            vmem((panels, depth, width), BF16),
            vmem((2 * mine, parents), BF16),
            vmem((n_col, mine, slots), F32),
            vmem((2 * n_rhs, slots), BF16),
            vmem((group, n_z, share, width), F32),
            vmem((group, n_z, share, width), F32),
            vmem((2 * sub, width), BF16),
            vmem((n_z, share, width), F32),
            vmem((n_z, share, width), F32),
            vmem((share, width), F32),
            vmem((panels, n_z, share, depth), F32),
            vmem((2 * sub, depth), BF16),
            dma,
            dma,
            dma((panels,)),
            dma((n_col,)),
            dma((n_col,)),
            dma((panels, group)),
            dma((panels, group)),
            dma((group,)),
            dma((group,)),
            dma((n_z,)),
            dma((n_z,)),
            dma((n_col, n_z)),
            dma((panels, n_z)),
        ],
        compiler_params=pltpu.CompilerParams(
            collective_id=0, has_side_effects=True, vmem_limit_bytes=52 * 1024 * 1024
        ),
        name="front_solve",
    )(slot_row[None, :], tile_count, anc_solution, rhs, anc_factor, lower_factor, diag_inverse)


def solution(mesh):
    in_specs = (
        P("row", "col"),
        P("col", "row"),
        P("row"),
        P("row"),
        P(None, "row", "col"),
        P("col", None, None),
        P("row", "col"),
    )
    body = functools.partial(on_device, mesh.shape["row"], mesh.shape["col"])
    return jax.shard_map(
        body, mesh=mesh, in_specs=in_specs, out_specs=P("row", "col"), check_vma=False
    )
```

time: 434 us -> 57.2 us (0.13)
  waiting for transfers between devices: 353 us -> 0 us
  Pallas kernels: 0 us -> 53.2 us
  matrix products: 30.3 us -> 0 us
  between operations: 14.2 us -> 0.67 us
  starting transfers between devices: 11.2 us -> 0 us
  other arithmetic: 10.5 us -> 0 us
  blocking collectives: 8.61 us -> 0 us
    reduce_scatter x4 -> x0, waiting for transfers between devices: 249 us -> none  [the longest x3 186 us: on_device(): lax.psum_scatter(partial_sum, 'row', scatter_dimension=0, tiled=True)]
    psum x3 -> x0, waiting for transfers between devices: 82.6 us -> none  [broadcast(): return lax.psum(jnp.where(mine, array, jnp.zeros_like(array)), axis)]
    pallas_call x0 -> x1, Pallas kernels: none -> 53.2 us  [on_device(): pl.pallas_call(functools.partial(kernel, group, n_row, n_col), out_shape=...]
    dot_general x8 -> x0, matrix products: 30.3 us -> none  [the longest x4 17.8 us: on_device(): jnp.dot(reduced - pending, diag_inverse[0], precision=highest, preferred_...]
    all_to_all x3 -> x0, waiting for transfers between devices: 20.6 us -> none  [on_device(): lax.all_to_all(solved, 'row', split_axis=1, concat_axis=0, tiled=True)]
    all_to_all x3 -> x0, starting transfers between devices: 10.8 us -> none  [on_device(): lax.all_to_all(solved, 'row', split_axis=1, concat_axis=0, tiled=True)]
    all_gather x1 -> x0, blocking collectives: 8.61 us -> none  [on_device(): lax.all_gather(selected, 'col', axis=0, tiled=True)]
  transfers between devices with their start and end apart: 10 -> 0, of which waited for: 10 -> 0; matrix products, arithmetic and copies ran while one was open for 1% -> 0% of each run, Pallas kernels for 0% -> 0%
where the time goes in v1:
time: 57.2 us; the launch traced here: 56.9 us
  Pallas kernels  53.2 us (93%)
  local copies, waits for them, and re-layouts  3.08 us (5%)
  between operations  0.67 us (1%)
    pallas_call x1, Pallas kernels, on_device(): pl.pallas_call(functools.partial(kernel, group, n_row, n_col), out_shape=...  53.2 us
    unnamed x7, local copies, waits for them, and re-layouts  3.08 us

profile of v1, /device:TPU:0, one launch (start us, length us, event | category | flops | bytes accessed | tf_op | source)
XLA Modules:
  0.0 56.9 jit_solution(8898470959284599042)
XLA Ops:
  0.7 0.0 copy-start
  0.7 0.9 %copy-done = f32[32,1536]{1,0:T(8,128)S(1)} copy-done((f32[32,1536]{1,0:T(8,128)S(1)}, f32[32,1536]{1,0:T(8,128)}, u32[]{:S(2)}) %copy-start) | copy-done | bytes 196632
  1.6 0.0 copy-start.1
  1.6 0.8 %copy-done.1 = f32[16,1024]{1,0:T(8,128)S(1)} copy-done((f32[16,1024]{1,0:T(8,128)S(1)}, f32[16,1024]{1,0:T(8,128)}, u32[]{:S(2)}) %copy-start.1) | copy-done | bytes 65560
  2.4 0.0 copy-start.2
  2.4 0.7 %copy-done.2 = s32[1024]{0:T(1024)S(1)} copy-done((s32[1024]{0:T(1024)S(1)}, s32[1024]{0:T(1024)}, u32[]{:S(2)}) %copy-start.2) | copy-done | bytes 4120
  3.1 53.2 %front_solve.1 = f32[16,1024]{1,0:T(8,128)S(1)} custom-call(s32[1,1024]{1,0:T(1,128)S(1)} %bitcast.1, s32[1]{0:T(128)S(6)} %copy.9.count_ref, f32[32,1536]{1,0:T(8,128)S(1)} %copy-done, f32[16,1024]{1,0:T(8,128)S(1)} %copy-done.1, f32[1024,1024]{1,0:T(8,128)} %anc_ref.1, f32[4,128,1024]{2,1,0:T(8,128)} %low_ref.1, f32[1,1024,1024]{2,1,0:T(8,128)} %diag_ref.1), custom_call_target="tpu_custom_call" | custom-call | tf_op jit(solution)/shard_map/front_solve/pallas_call | solution.py:334
  56.3 0.6 %copy.10 = f32[16,1024]{1,0:T(8,128)} copy(f32[16,1024]{1,0:T(8,128)S(1)} %front_solve.1) | data formatting | bytes 131072
Async XLA Ops:
  0.7 0.9 %copy-start = (f32[32,1536]{1,0:T(8,128)S(1)}, f32[32,1536]{1,0:T(8,128)}, u32[]{:S(2)}) copy-start(f32[32,1536]{1,0:T(8,128)} %parent_ref.1) | copy-start | bytes 589828
  1.6 0.8 %copy-start.1 = (f32[16,1024]{1,0:T(8,128)S(1)}, f32[16,1024]{1,0:T(8,128)}, u32[]{:S(2)}) copy-start(f32[16,1024]{1,0:T(8,128)} %rhs_ref.1) | copy-start | bytes 196612
  2.4 0.7 %copy-start.2 = (s32[1024]{0:T(1024)S(1)}, s32[1024]{0:T(1024)}, u32[]{:S(2)}) copy-start(s32[1024]{0:T(1024)} %param.9) | copy-start | bytes 12292

commit v2 on v1

--- a/solution.py
+++ b/solution.py
@@ -28,14 +28,17 @@
     group,
     n_row,
     n_col,
-    slot_ref,
     count_ref,
-    parent_ref,
-    rhs_ref,
+    slot_hbm,
+    parent_hbm,
+    rhs_hbm,
     anc_ref,
     low_ref,
     diag_ref,
     out_ref,
+    slot_ref,
+    parent_ref,
+    rhs_ref,
     anc_f,
     anc_h,
     anc_l,
@@ -57,10 +60,12 @@
     solved,
     x_in,
     x_s,
+    sem_in,
     sem_anc,
     sem_diag,
     sem_low,
     sel_tx,
+    fwd_tx,
     sel_rx,
     low_tx,
     low_rx,
@@ -85,6 +90,12 @@
     steps = width // wide
     depth = x_in.shape[3]
 
+    copy_slot = pltpu.make_async_copy(slot_hbm, slot_ref, sem_in.at[0])
+    copy_slot.start()
+    copy_parent = pltpu.make_async_copy(parent_hbm, parent_ref, sem_in.at[1])
+    copy_parent.start()
+    copy_rhs = pltpu.make_async_copy(rhs_hbm, rhs_ref, sem_in.at[2])
+    copy_rhs.start()
     copy_anc = pltpu.make_async_copy(anc_ref, anc_f, sem_anc)
     copy_anc.start()
     copy_diag = pltpu.make_async_copy(diag_ref.at[0], diag_f, sem_diag)
@@ -105,40 +116,44 @@
         greet(z * group + lax.rem(y + d, group), col)
 
     mine = sel.shape[1]
+    picks = slots // wide
+    core = lax.rem(col, 2)
+    sibling = col + 1 - 2 * core
+
+    def sel_copy(owner, n, to, tx):
+        at = slice(n * wide, (n + 1) * wide)
+        return pltpu.make_async_remote_copy(
+            src_ref=sel.at[owner, :, at],
+            dst_ref=sel.at[owner, :, at],
+            send_sem=tx,
+            recv_sem=sel_rx.at[owner, n],
+            device_id=(row, to),
+            device_id_type=MESH,
+        )
+
+    def far_col(e):
+        return lax.rem(col + 2 * e, n_col)
+
+    far = n_col // 2
+    copy_slot.wait()
+    copy_parent.wait()
     hi, lo = split(parent_ref[...])
     par_s[0:mine, :] = hi
     par_s[mine:, :] = lo
     parents = parent_ref.shape[1]
-
-    def select(n, carry):
-        at = pl.ds(pl.multiple_of(n * wide, wide), wide)
+    for n in range(picks):
+        at = slice(n * wide, (n + 1) * wide)
         place = lax.broadcasted_iota(jnp.int32, (1, wide), 1) + n * wide
         wanted = jnp.where(place < count_ref[0] * TILE, slot_ref[:, at], -1)
         which = lax.broadcasted_iota(jnp.int32, (parents, wide), 0)
         hot = jnp.where(which == wanted, 1.0, 0.0).astype(BF16)
         both = mm(par_s[...], hot)
         sel[col, :, at] = both[0:mine] + both[mine:]
-        return carry
-
-    lax.fori_loop(0, slots // wide, select, 0)
-
-    pl.semaphore_wait(barrier, n_z * n_col - 1 + group - 1)
-
-    def sel_copy(owner, to):
-        return pltpu.make_async_remote_copy(
-            src_ref=sel.at[owner],
-            dst_ref=sel.at[owner],
-            send_sem=sel_tx.at[to],
-            recv_sem=sel_rx.at[owner],
-            device_id=(row, to),
-            device_id_type=MESH,
-        )
-
-    def others_col(e):
-        return lax.rem(col + e, n_col)
-
-    for e in range(1, n_col):
-        sel_copy(col, others_col(e)).start()
+        if n == 0:
+            pl.semaphore_wait(barrier, n_z * n_col - 1 + group - 1)
+        for e in range(1, far):
+            sel_copy(col, n, far_col(e), sel_tx.at[far_col(e), n]).start()
+        sel_copy(col, n, sibling, sel_tx.at[sibling, n]).start()
 
     def low_copy(k, owner, to):
         return pltpu.make_async_remote_copy(
@@ -171,52 +186,76 @@
 
     copy_anc.wait()
     split_rows(anc_f, anc_h, anc_l)
-
-    for e in range(1, n_col):
-        sel_copy(others_col(e), col).wait_recv()
+    for n in range(picks):
+        for e in range(1, far):
+            owner = far_col(e)
+            sel_copy(owner, n, col, sel_tx.at[col, n]).wait_recv()
+            sel_copy(owner, n, sibling, fwd_tx.at[owner, n]).start()
+    copy_diag.wait()
+    split_rows(diag_f, diag_h, diag_l)
+    for n in range(picks):
+        for e in range(far):
+            owner = lax.rem(sibling + 2 * e, n_col)
+            sel_copy(owner, n, col, sel_tx.at[col, n]).wait_recv()
     hi, lo = split(sel[...].reshape(n_rhs, slots))
     sel_s[0:n_rhs, :] = hi
     sel_s[n_rhs:, :] = lo
-    for n in range(steps):
+    def part_copy(owner, to, n):
+        at = slice(n * wide, (n + 1) * wide)
+        return pltpu.make_async_remote_copy(
+            src_ref=part.at[to, :, :, at],
+            dst_ref=part_in.at[owner, :, :, at],
+            send_sem=part_tx.at[to, n],
+            recv_sem=part_rx.at[owner, n],
+            device_id=(z * group + to, col),
+            device_id_type=MESH,
+        )
+
+    def red_copy(owner, to, n):
+        at = slice(n * wide, (n + 1) * wide)
+        return pltpu.make_async_remote_copy(
+            src_ref=acc.at[to, :, at],
+            dst_ref=red_in.at[owner, :, at],
+            send_sem=red_tx.at[to, n],
+            recv_sem=red_rx.at[owner, n],
+            device_id=(to * group + y, col),
+            device_id_type=MESH,
+        )
+
+    def send_sums(n):
+        for d in range(1, n_z):
+            red_copy(z, lax.rem(z + d, n_z), n).start()
+
+    order = range(steps - 1, -1, -1)
+    for n in order:
         at = slice(n * wide, (n + 1) * wide)
         both = mm(sel_s[...], anc_h[:, at])
         term = both[0:n_rhs] + both[n_rhs:] + mm(sel_s[0:n_rhs, :], anc_l[:, at])
         for r in range(n_row):
             part[r % group, r // group, :, at] = term[r * share : (r + 1) * share]
-
-    def part_copy(owner, to):
-        return pltpu.make_async_remote_copy(
-            src_ref=part.at[to],
-            dst_ref=part_in.at[owner],
-            send_sem=part_tx.at[to],
-            recv_sem=part_rx.at[owner],
-            device_id=(z * group + to, col),
-            device_id_type=MESH,
-        )
-
-    for d in range(1, group):
-        part_copy(y, lax.rem(y + d, group)).start()
-
-    copy_diag.wait()
-    split_rows(diag_f, diag_h, diag_l)
-
-    for d in range(1, group):
-        part_copy(lax.rem(y + d, group), y).wait_recv()
-
-    pre = part[y]
-    for d in range(1, group):
-        pre = pre + part_in[lax.rem(y + d, group)]
+        for d in range(1, group):
+            part_copy(y, lax.rem(y + d, group), n).start()
+
+    copy_rhs.wait()
     zs = lax.broadcasted_iota(jnp.int32, (n_z, 1, 1), 0)
-    pre = jnp.where(zs == z, rhs_ref[...][None], 0.0) - pre
-    hi, lo = split(pre.reshape(sub, width))
-    pre_s[0:sub, :] = hi
-    pre_s[sub:, :] = lo
-    for n in range(steps):
+    for n in order:
         at = slice(n * wide, (n + 1) * wide)
         below = slice(n * wide, width)
+        pre = jnp.where(zs == z, rhs_ref[:, at][None], 0.0) - part[y, :, :, at]
+        for d in range(1, group):
+            owner = lax.rem(y + d, group)
+            part_copy(owner, y, n).wait_recv()
+            pre = pre - part_in[owner, :, :, at]
+        hi, lo = split(pre.reshape(sub, wide))
+        pre_s[0:sub, at] = hi
+        pre_s[sub:, at] = lo
         both = mm(pre_s[:, below], diag_h[below, at])
         term = both[0:sub] + both[sub:] + mm(pre_s[0:sub, below], diag_l[below, at])
         acc[:, :, at] = term.reshape(n_z, share, wide)
+
+        @pl.when(col == n_col - 1)
+        def _():
+            send_sums(n)
 
     for k in range(1, n_col):
         pltpu.make_async_copy(low_ref.at[k], low_all.at[k, y], sem_low.at[k]).wait()
@@ -257,56 +296,60 @@
         h, l = split(x_in[k].reshape(sub, depth))
         x_s[0:sub, :] = h
         x_s[sub:, :] = l
-        for n in range(steps):
+        for n in order:
             at = slice(n * wide, (n + 1) * wide)
             both = mm(x_s[...], fold_h[k, :, at])
             term = both[0:sub] + both[sub:] + mm(x_s[0:sub, :], fold_l[k, :, at])
             acc[:, :, at] = acc[:, :, at] - term.reshape(n_z, share, wide)
+
+            @pl.when(k == col + 1)
+            def _():
+                send_sums(n)
+
         return carry
 
     lax.fori_loop(0, n_col - 1 - col, absorb, 0)
 
-    def red_copy(owner, to):
-        return pltpu.make_async_remote_copy(
-            src_ref=acc.at[to],
-            dst_ref=red_in.at[owner],
-            send_sem=red_tx.at[to],
-            recv_sem=red_rx.at[owner],
-            device_id=(to * group + y, col),
-            device_id_type=MESH,
-        )
-
-    for d in range(1, n_z):
-        red_copy(z, lax.rem(z + d, n_z)).start()
-    total = acc[z]
-    for d in range(1, n_z):
-        at = lax.rem(z + d, n_z)
-        red_copy(at, z).wait_recv()
-        total = total + red_in[at]
-    solved[...] = total
+    per = wide // depth
+    for n in order:
+        at = slice(n * wide, (n + 1) * wide)
+        total = acc[z, :, at]
+        for d in range(1, n_z):
+            owner = lax.rem(z + d, n_z)
+            red_copy(owner, z, n).wait_recv()
+            total = total + red_in[owner, :, at]
+        solved[:, at] = total
+
+        @pl.when(col > 0)
+        def _():
+            for to in range(n * per, (n + 1) * per):
+                x_copy(col, z, to, col - 1).start()
 
     def spread(i, carry):
-        to_col = col - 1 - i
-        for d in range(n_z):
-            x_copy(col, z, lax.rem(z + d, n_z), to_col).start()
+        for to in range(n_z):
+            x_copy(col, z, to, col - 2 - i).start()
         return carry
 
-    lax.fori_loop(0, col, spread, 0)
-    out_ref[...] = total
+    lax.fori_loop(0, col - 1, spread, 0)
+    out_ref[...] = solved[...]
 
     def spread_done(i, carry):
-        to_col = col - 1 - i
-        for d in range(n_z):
-            x_copy(col, z, lax.rem(z + d, n_z), to_col).wait_send()
+        for to in range(n_z):
+            x_copy(col, z, to, col - 1 - i).wait_send()
         return carry
 
     lax.fori_loop(0, col, spread_done, 0)
-    for d in range(1, n_z):
-        red_copy(z, lax.rem(z + d, n_z)).wait_send()
-    for d in range(1, group):
-        part_copy(y, lax.rem(y + d, group)).wait_send()
-    for e in range(1, n_col):
-        sel_copy(col, others_col(e)).wait_send()
+    for n in range(steps):
+        for d in range(1, n_z):
+            red_copy(z, lax.rem(z + d, n_z), n).wait_send()
+        for d in range(1, group):
+            part_copy(y, lax.rem(y + d, group), n).wait_send()
+    for n in range(picks):
+        for e in range(1, far):
+            owner = far_col(e)
+            sel_copy(col, n, owner, sel_tx.at[owner, n]).wait_send()
+            sel_copy(owner, n, sibling, fwd_tx.at[owner, n]).wait_send()
+        sel_copy(col, n, sibling, sel_tx.at[sibling, n]).wait_send()
     for k in range(n_col - 1, 0, -1):
 
         @pl.when(col < k)
@@ -327,6 +370,8 @@
     depth = group * rows_local
     sub = share * n_z
     mine, parents = anc_solution.shape
+    wide = min(256, width)
+    picks, steps = slots // wide, width // wide
     dma = pltpu.SemaphoreType.DMA
     vmem = pltpu.VMEM
     in_vmem = pl.BlockSpec(memory_space=pltpu.VMEM)
@@ -335,16 +380,19 @@
         functools.partial(kernel, group, n_row, n_col),
         out_shape=jax.ShapeDtypeStruct(rhs.shape, F32),
         in_specs=[
-            in_vmem,
             pl.BlockSpec(memory_space=pltpu.SMEM),
-            in_vmem,
-            in_vmem,
+            anywhere,
+            anywhere,
+            anywhere,
             anywhere,
             anywhere,
             anywhere,
         ],
         out_specs=in_vmem,
         scratch_shapes=[
+            vmem((1, slots), jnp.int32),
+            vmem((mine, parents), F32),
+            vmem(rhs.shape, F32),
             vmem((slots, width), F32),
             vmem((slots, width), BF16),
             vmem((slots, width), BF16),
@@ -366,17 +414,19 @@
             vmem((share, width), F32),
             vmem((panels, n_z, share, depth), F32),
             vmem((2 * sub, depth), BF16),
+            dma((3,)),
             dma,
             dma,
             dma((panels,)),
-            dma((n_col,)),
-            dma((n_col,)),
+            dma((n_col, picks)),
+            dma((n_col, picks)),
+            dma((n_col, picks)),
             dma((panels, group)),
             dma((panels, group)),
-            dma((group,)),
-            dma((group,)),
-            dma((n_z,)),
-            dma((n_z,)),
+            dma((group, steps)),
+            dma((group, steps)),
+            dma((n_z, steps)),
+            dma((n_z, steps)),
             dma((n_col, n_z)),
             dma((panels, n_z)),
         ],
@@ -384,7 +434,7 @@
             collective_id=0, has_side_effects=True, vmem_limit_bytes=52 * 1024 * 1024
         ),
         name="front_solve",
-    )(slot_row[None, :], tile_count, anc_solution, rhs, anc_factor, lower_factor, diag_inverse)
+    )(tile_count, slot_row[None, :], anc_solution, rhs, anc_factor, lower_factor, diag_inverse)
 
 
 def solution(mesh):

time: 57.2 us -> 59.9 us (1.047)
  Pallas kernels: 53.2 us -> 55.9 us
    pallas_call x1, Pallas kernels: 53.2 us -> 55.9 us  [on_device(): pl.pallas_call(functools.partial(kernel, group, n_row, n_col), out_shape=...]
where the time goes in v2:
time: 59.9 us; the launch traced here: 59.7 us
  Pallas kernels  55.9 us (93%)
  local copies, waits for them, and re-layouts  3.08 us (5%)
  between operations  0.67 us (1%)
    pallas_call x1, Pallas kernels, on_device(): pl.pallas_call(functools.partial(kernel, group, n_row, n_col), out_shape=...  55.9 us
    unnamed x7, local copies, waits for them, and re-layouts  3.08 us

profile of v2, /device:TPU:0, one launch (start us, length us, event | category | flops | bytes accessed | tf_op | source)
XLA Modules:
  0.0 59.7 jit_solution(11709395901771748493)
XLA Ops:
  0.7 0.0 copy-start
  0.7 0.9 %copy-done = f32[32,1536]{1,0:T(8,128)S(1)} copy-done((f32[32,1536]{1,0:T(8,128)S(1)}, f32[32,1536]{1,0:T(8,128)}, u32[]{:S(2)}) %copy-start) | copy-done | bytes 196632
  1.6 0.0 copy-start.1
  1.6 0.8 %copy-done.1 = f32[16,1024]{1,0:T(8,128)S(1)} copy-done((f32[16,1024]{1,0:T(8,128)S(1)}, f32[16,1024]{1,0:T(8,128)}, u32[]{:S(2)}) %copy-start.1) | copy-done | bytes 65560
  2.4 0.0 copy-start.2
  2.4 0.7 %copy-done.2 = s32[1024]{0:T(1024)S(1)} copy-done((s32[1024]{0:T(1024)S(1)}, s32[1024]{0:T(1024)}, u32[]{:S(2)}) %copy-start.2) | copy-done | bytes 4120
  3.1 55.9 %front_solve.1 = f32[16,1024]{1,0:T(8,128)S(1)} custom-call(s32[1]{0:T(128)S(6)} %copy.9.count_ref, s32[1,1024]{1,0:T(1,128)S(1)} %bitcast.1, f32[32,1536]{1,0:T(8,128)S(1)} %copy-done, f32[16,1024]{1,0:T(8,128)S(1)} %copy-done.1, f32[1024,1024]{1,0:T(8,128)} %anc_ref.1, f32[4,128,1024]{2,1,0:T(8,128)} %low_ref.1, f32[1,1024,1024]{2,1,0:T(8,128)} %diag_ref.1), custom_call_target="tpu_custom_call" | custom-call | tf_op jit(solution)/shard_map/front_solve/pallas_call | solution.py:379
  59.0 0.6 %copy.10 = f32[16,1024]{1,0:T(8,128)} copy(f32[16,1024]{1,0:T(8,128)S(1)} %front_solve.1) | data formatting | bytes 131072
Async XLA Ops:
  0.7 0.9 %copy-start = (f32[32,1536]{1,0:T(8,128)S(1)}, f32[32,1536]{1,0:T(8,128)}, u32[]{:S(2)}) copy-start(f32[32,1536]{1,0:T(8,128)} %parent_hbm.1) | copy-start | bytes 589828
  1.6 0.8 %copy-start.1 = (f32[16,1024]{1,0:T(8,128)S(1)}, f32[16,1024]{1,0:T(8,128)}, u32[]{:S(2)}) copy-start(f32[16,1024]{1,0:T(8,128)} %rhs_hbm.1) | copy-start | bytes 196612
  2.4 0.7 %copy-start.2 = (s32[1024]{0:T(1024)S(1)}, s32[1024]{0:T(1024)}, u32[]{:S(2)}) copy-start(s32[1024]{0:T(1024)} %param.9) | copy-start | bytes 12292

commit v3 on v2

--- a/solution.py
+++ b/solution.py
@@ -115,45 +115,7 @@
     for d in range(1, group):
         greet(z * group + lax.rem(y + d, group), col)
 
-    mine = sel.shape[1]
-    picks = slots // wide
-    core = lax.rem(col, 2)
-    sibling = col + 1 - 2 * core
-
-    def sel_copy(owner, n, to, tx):
-        at = slice(n * wide, (n + 1) * wide)
-        return pltpu.make_async_remote_copy(
-            src_ref=sel.at[owner, :, at],
-            dst_ref=sel.at[owner, :, at],
-            send_sem=tx,
-            recv_sem=sel_rx.at[owner, n],
-            device_id=(row, to),
-            device_id_type=MESH,
-        )
-
-    def far_col(e):
-        return lax.rem(col + 2 * e, n_col)
-
-    far = n_col // 2
-    copy_slot.wait()
-    copy_parent.wait()
-    hi, lo = split(parent_ref[...])
-    par_s[0:mine, :] = hi
-    par_s[mine:, :] = lo
-    parents = parent_ref.shape[1]
-    for n in range(picks):
-        at = slice(n * wide, (n + 1) * wide)
-        place = lax.broadcasted_iota(jnp.int32, (1, wide), 1) + n * wide
-        wanted = jnp.where(place < count_ref[0] * TILE, slot_ref[:, at], -1)
-        which = lax.broadcasted_iota(jnp.int32, (parents, wide), 0)
-        hot = jnp.where(which == wanted, 1.0, 0.0).astype(BF16)
-        both = mm(par_s[...], hot)
-        sel[col, :, at] = both[0:mine] + both[mine:]
-        if n == 0:
-            pl.semaphore_wait(barrier, n_z * n_col - 1 + group - 1)
-        for e in range(1, far):
-            sel_copy(col, n, far_col(e), sel_tx.at[far_col(e), n]).start()
-        sel_copy(col, n, sibling, sel_tx.at[sibling, n]).start()
+    pl.semaphore_wait(barrier, n_z * n_col - 1 + group - 1)
 
     def low_copy(k, owner, to):
         return pltpu.make_async_remote_copy(
@@ -171,6 +133,44 @@
         def _():
             for d in range(1, group):
                 low_copy(k, y, lax.rem(y + d, group)).start()
+
+    mine = sel.shape[1]
+    picks = slots // wide
+    core = lax.rem(col, 2)
+    sibling = col + 1 - 2 * core
+
+    def sel_copy(owner, n, to, tx):
+        at = slice(n * wide, (n + 1) * wide)
+        return pltpu.make_async_remote_copy(
+            src_ref=sel.at[owner, :, at],
+            dst_ref=sel.at[owner, :, at],
+            send_sem=tx,
+            recv_sem=sel_rx.at[owner, n],
+            device_id=(row, to),
+            device_id_type=MESH,
+        )
+
+    def far_col(e):
+        return lax.rem(col + 2 * e, n_col)
+
+    far = n_col // 2
+    copy_slot.wait()
+    copy_parent.wait()
+    hi, lo = split(parent_ref[...])
+    par_s[0:mine, :] = hi
+    par_s[mine:, :] = lo
+    parents = parent_ref.shape[1]
+    for n in range(picks):
+        at = slice(n * wide, (n + 1) * wide)
+        place = lax.broadcasted_iota(jnp.int32, (1, wide), 1) + n * wide
+        wanted = jnp.where(place < count_ref[0] * TILE, slot_ref[:, at], -1)
+        which = lax.broadcasted_iota(jnp.int32, (parents, wide), 0)
+        hot = jnp.where(which == wanted, 1.0, 0.0).astype(BF16)
+        both = mm(par_s[...], hot)
+        sel[col, :, at] = both[0:mine] + both[mine:]
+        for e in range(1, far):
+            sel_copy(col, n, far_col(e), sel_tx.at[far_col(e), n]).start()
+        sel_copy(col, n, sibling, sel_tx.at[sibling, n]).start()
 
     def split_rows(src, dst_h, dst_l):
         rows = 128

time: 59.9 us -> 58.8 us (0.982)
  Pallas kernels: 55.9 us -> 54.9 us
    pallas_call x1, Pallas kernels: 55.9 us -> 54.9 us  [on_device(): pl.pallas_call(functools.partial(kernel, group, n_row, n_col), out_shape=...]
where the time goes in v3:
time: 58.8 us; the launch traced here: 58.6 us
  Pallas kernels  54.9 us (93%)
  local copies, waits for them, and re-layouts  3.08 us (5%)
  between operations  0.67 us (1%)
    pallas_call x1, Pallas kernels, on_device(): pl.pallas_call(functools.partial(kernel, group, n_row, n_col), out_shape=...  54.9 us
    unnamed x7, local copies, waits for them, and re-layouts  3.08 us

profile of v3, /device:TPU:0, one launch (start us, length us, event | category | flops | bytes accessed | tf_op | source)
XLA Modules:
  0.0 58.6 jit_solution(14517034053986144229)
XLA Ops:
  0.7 0.0 copy-start
  0.7 0.9 %copy-done = f32[32,1536]{1,0:T(8,128)S(1)} copy-done((f32[32,1536]{1,0:T(8,128)S(1)}, f32[32,1536]{1,0:T(8,128)}, u32[]{:S(2)}) %copy-start) | copy-done | bytes 196632
  1.6 0.0 copy-start.1
  1.6 0.8 %copy-done.1 = f32[16,1024]{1,0:T(8,128)S(1)} copy-done((f32[16,1024]{1,0:T(8,128)S(1)}, f32[16,1024]{1,0:T(8,128)}, u32[]{:S(2)}) %copy-start.1) | copy-done | bytes 65560
  2.4 0.0 copy-start.2
  2.4 0.7 %copy-done.2 = s32[1024]{0:T(1024)S(1)} copy-done((s32[1024]{0:T(1024)S(1)}, s32[1024]{0:T(1024)}, u32[]{:S(2)}) %copy-start.2) | copy-done | bytes 4120
  3.1 54.9 %front_solve.1 = f32[16,1024]{1,0:T(8,128)S(1)} custom-call(s32[1]{0:T(128)S(6)} %copy.9.count_ref, s32[1,1024]{1,0:T(1,128)S(1)} %bitcast.1, f32[32,1536]{1,0:T(8,128)S(1)} %copy-done, f32[16,1024]{1,0:T(8,128)S(1)} %copy-done.1, f32[1024,1024]{1,0:T(8,128)} %anc_ref.1, f32[4,128,1024]{2,1,0:T(8,128)} %low_ref.1, f32[1,1024,1024]{2,1,0:T(8,128)} %diag_ref.1), custom_call_target="tpu_custom_call" | custom-call | tf_op jit(solution)/shard_map/front_solve/pallas_call | solution.py:379
  58.0 0.6 %copy.10 = f32[16,1024]{1,0:T(8,128)} copy(f32[16,1024]{1,0:T(8,128)S(1)} %front_solve.1) | data formatting | bytes 131072
Async XLA Ops:
  0.7 0.9 %copy-start = (f32[32,1536]{1,0:T(8,128)S(1)}, f32[32,1536]{1,0:T(8,128)}, u32[]{:S(2)}) copy-start(f32[32,1536]{1,0:T(8,128)} %parent_hbm.1) | copy-start | bytes 589828
  1.6 0.8 %copy-start.1 = (f32[16,1024]{1,0:T(8,128)S(1)}, f32[16,1024]{1,0:T(8,128)}, u32[]{:S(2)}) copy-start(f32[16,1024]{1,0:T(8,128)} %rhs_hbm.1) | copy-start | bytes 196612
  2.4 0.7 %copy-start.2 = (s32[1024]{0:T(1024)S(1)}, s32[1024]{0:T(1024)}, u32[]{:S(2)}) copy-start(s32[1024]{0:T(1024)} %param.9) | copy-start | bytes 12292

commit v4 on v1

--- a/solution.py
+++ b/solution.py
@@ -104,6 +104,25 @@
     for d in range(1, group):
         greet(z * group + lax.rem(y + d, group), col)
 
+    pl.semaphore_wait(barrier, n_z * n_col - 1 + group - 1)
+
+    def low_copy(k, owner, to):
+        return pltpu.make_async_remote_copy(
+            src_ref=low_ref.at[k],
+            dst_ref=low_all.at[k, owner],
+            send_sem=low_tx.at[k, to],
+            recv_sem=low_rx.at[k, owner],
+            device_id=(z * group + to, col),
+            device_id_type=MESH,
+        )
+
+    for k in range(n_col - 1, 0, -1):
+
+        @pl.when(col < k)
+        def _():
+            for d in range(1, group):
+                low_copy(k, y, lax.rem(y + d, group)).start()
+
     mine = sel.shape[1]
     hi, lo = split(parent_ref[...])
     par_s[0:mine, :] = hi
@@ -122,8 +141,6 @@
 
     lax.fori_loop(0, slots // wide, select, 0)
 
-    pl.semaphore_wait(barrier, n_z * n_col - 1 + group - 1)
-
     def sel_copy(owner, to):
         return pltpu.make_async_remote_copy(
             src_ref=sel.at[owner],
@@ -139,23 +156,6 @@
 
     for e in range(1, n_col):
         sel_copy(col, others_col(e)).start()
-
-    def low_copy(k, owner, to):
-        return pltpu.make_async_remote_copy(
-            src_ref=low_ref.at[k],
-            dst_ref=low_all.at[k, owner],
-            send_sem=low_tx.at[k, to],
-            recv_sem=low_rx.at[k, owner],
-            device_id=(z * group + to, col),
-            device_id_type=MESH,
-        )
-
-    for k in range(n_col - 1, 0, -1):
-
-        @pl.when(col < k)
-        def _():
-            for d in range(1, group):
-                low_copy(k, y, lax.rem(y + d, group)).start()
 
     def split_rows(src, dst_h, dst_l):
         rows = 128

time: 57.2 us -> 57.4 us (level)
  no operation moved by 1% of the time
where the time goes in v4:
time: 57.4 us; the launch traced here: 57.2 us
  Pallas kernels  53.4 us (93%)
  local copies, waits for them, and re-layouts  3.08 us (5%)
  between operations  0.67 us (1%)
    pallas_call x1, Pallas kernels, on_device(): pl.pallas_call(functools.partial(kernel, group, n_row, n_col), out_shape=...  53.4 us
    unnamed x7, local copies, waits for them, and re-layouts  3.08 us

profile of v4, /device:TPU:0, one launch (start us, length us, event | category | flops | bytes accessed | tf_op | source)
XLA Modules:
  0.0 57.2 jit_solution(995665923657526865)
XLA Ops:
  0.7 0.0 copy-start
  0.7 0.9 %copy-done = f32[32,1536]{1,0:T(8,128)S(1)} copy-done((f32[32,1536]{1,0:T(8,128)S(1)}, f32[32,1536]{1,0:T(8,128)}, u32[]{:S(2)}) %copy-start) | copy-done | bytes 196632
  1.6 0.0 copy-start.1
  1.6 0.8 %copy-done.1 = f32[16,1024]{1,0:T(8,128)S(1)} copy-done((f32[16,1024]{1,0:T(8,128)S(1)}, f32[16,1024]{1,0:T(8,128)}, u32[]{:S(2)}) %copy-start.1) | copy-done | bytes 65560
  2.4 0.0 copy-start.2
  2.4 0.7 %copy-done.2 = s32[1024]{0:T(1024)S(1)} copy-done((s32[1024]{0:T(1024)S(1)}, s32[1024]{0:T(1024)}, u32[]{:S(2)}) %copy-start.2) | copy-done | bytes 4120
  3.1 53.4 %front_solve.1 = f32[16,1024]{1,0:T(8,128)S(1)} custom-call(s32[1,1024]{1,0:T(1,128)S(1)} %bitcast.1, s32[1]{0:T(128)S(6)} %copy.9.count_ref, f32[32,1536]{1,0:T(8,128)S(1)} %copy-done, f32[16,1024]{1,0:T(8,128)S(1)} %copy-done.1, f32[1024,1024]{1,0:T(8,128)} %anc_ref.1, f32[4,128,1024]{2,1,0:T(8,128)} %low_ref.1, f32[1,1024,1024]{2,1,0:T(8,128)} %diag_ref.1), custom_call_target="tpu_custom_call" | custom-call | tf_op jit(solution)/shard_map/front_solve/pallas_call | solution.py:334
  56.5 0.6 %copy.10 = f32[16,1024]{1,0:T(8,128)} copy(f32[16,1024]{1,0:T(8,128)S(1)} %front_solve.1) | data formatting | bytes 131072
Async XLA Ops:
  0.7 0.9 %copy-start = (f32[32,1536]{1,0:T(8,128)S(1)}, f32[32,1536]{1,0:T(8,128)}, u32[]{:S(2)}) copy-start(f32[32,1536]{1,0:T(8,128)} %parent_ref.1) | copy-start | bytes 589828
  1.6 0.8 %copy-start.1 = (f32[16,1024]{1,0:T(8,128)S(1)}, f32[16,1024]{1,0:T(8,128)}, u32[]{:S(2)}) copy-start(f32[16,1024]{1,0:T(8,128)} %rhs_ref.1) | copy-start | bytes 196612
  2.4 0.7 %copy-start.2 = (s32[1024]{0:T(1024)S(1)}, s32[1024]{0:T(1024)}, u32[]{:S(2)}) copy-start(s32[1024]{0:T(1024)} %param.9) | copy-start | bytes 12292
